TPU v7x, 256 devices: a whole 4x4x8 slice. The times are simulated.
256 devices in a mesh: dp: 64 (over z_lo, y, x), mp: 4 (over z_hi, core).
Axes of the slice: x: 4, y: 4, z: 8 (z_hi: 2, z_lo: 4; z = z_hi * 4 + z_lo), core: 2. Of those that a mesh axis runs over, the one named last changes fastest.
Arguments:
- tokens: bfloat16 [16384, 8192], P('dp', 'mp'), may hold values from -8 to 8
- attn_gain: bfloat16 [8192], replicated, may hold values from 0.5 to 1.5
- w_query: bfloat16 [8192, 4096], P('dp', 'mp'), may hold values from -2 to 2
- key_projection_weight: bfloat16 [8192, 512], P('dp', 'mp'), may hold values from -2 to 2
- value_projection_weight: bfloat16 [8192, 512], P('dp', 'mp'), may hold values from -0.0625 to 0.0625
- w_out: bfloat16 [4096, 8192], P('mp', 'dp'), may hold values from -0.09375 to 0.09375
- final_gain: bfloat16 [8192], P('mp'), may hold values from 0.5 to 1.5
- unembed: bfloat16 [64128, 8192], P('dp', 'mp'), may hold values from -0.29882812 to 0.29882812
- clean_ids: int32 [64], replicated, may hold values from 0 to 64127, as said below
- corrupt_ids: int32 [64], replicated, may hold values from 0 to 64127
Outputs:
- head_out: bfloat16 [16384, 4096], P('dp', 'mp')
- scores: float32 [64, 32], P('dp', 'mp')
- metric: float32 [64], P('dp')
Inputs may be any that keep to these rules, and one draw needn't show every extreme that they name: `clean_ids`: split the ids into 64 aligned blocks of equal size and number the groups of 1 sequence alike; the block of a clean answer, minus the number of its sequence's group, taken modulo the number of blocks, is drawn so that every such offset occurs for some sequence.
All inputs are finite; a program needn't handle non-finite values.
Results may differ from a plain program's by a relative error of at most 0.015.
Values may be sent and summed in bfloat16 or wider, within the bound.
No kernel may reach another device: no remote copies, remote signals or barrier semaphores. Data moves between devices by JAX's collectives and lax.ppermute only.
A program may use at most 128 MiB of HBM per device.

v0:
```python
import math
import jax
import jax.numpy as jnp
from jax import lax
from jax.sharding import Mesh, PartitionSpec as P

MODEL_WIDTH = 8192
HEAD_SIZE = 128
LENGTH = 256
TOKENS = 16384
DP = ("zl", "y", "x")
MP = ("zh", "c")
F32 = jnp.float32
BF16 = jnp.bfloat16


def from_everyone(value, axis):
    count = lax.axis_size(axis)
    return lax.all_to_all(
        jnp.broadcast_to(value[None], (count, *value.shape)), axis, 0, 0, tiled=True
    )


def send(value, route):
    pairs = []
    for x in range(4):
        for c in range(2):
            to = route(x, c)
            if to is not None:
                pairs.append((x * 2 + c, to[0] % 4 * 2 + to[1]))
    return lax.ppermute(value, ("x", "c"), pairs)


def rotary_tables():
    half = HEAD_SIZE // 2
    positions = jnp.arange(LENGTH, dtype=F32)
    inv_freq = jnp.exp(jnp.arange(half, dtype=F32) * (-2.0 * math.log(500000.0) / HEAD_SIZE))
    angles = positions[:, None] * inv_freq[None, :]
    return (jnp.cos(angles)[:, None, :], jnp.sin(angles)[:, None, :])


def rotate(t, cos, sin):
    half = HEAD_SIZE // 2
    lo, hi = (t[..., :half], t[..., half:])
    return jnp.concatenate([lo * cos - hi * sin, hi * cos + lo * sin], axis=-1)


def ring_share(block, core):
    pa = send(block, lambda x, c: (x - 1, 0) if c == 0 else (x + 1, 1))
    pb = send(block, lambda x, c: (x + 1, 1) if c == 0 else (x - 1, 0))
    pc = send(block, lambda x, c: (x + 2, 1) if c == 0 else (x, 0))
    pd = send(block, lambda x, c: None if c == 0 else (x + 2, 1))
    first = core == 0
    f0 = jnp.concatenate([jnp.where(first, block, pc), jnp.where(first, pa, pb)], axis=0)
    f1 = jnp.concatenate([jnp.where(first, pc, pd), jnp.where(first, pb, pa)], axis=0)
    return (f0, f1)


def per_device(tokens, gain, w_query, w_key, w_value, w_out, final_gain, unembed, clean, corrupt):
    zh, core, x = (lax.axis_index("zh"), lax.axis_index("c"), lax.axis_index("x"))
    odd = x % 2
    with jax.named_scope("weights"):
        wkv = jnp.concatenate([w_key, w_value], axis=1)
        width = w_query.shape[1] // 2
        mine = lax.dynamic_slice_in_dim(w_query, odd * width, width, 1)
        other = lax.dynamic_slice_in_dim(w_query, (1 - odd) * width, width, 1)
        pa = send(jnp.concatenate([mine, wkv], axis=1), lambda x, c: (2 * c + x % 2, x // 2))
        pb = send(jnp.concatenate([other, wkv], axis=1), lambda x, c: (2 * c + 1 - x % 2, x // 2))
        rows = jnp.concatenate([jnp.where(odd == 0, pa, pb), jnp.where(odd == 0, pb, pa)], axis=0)
        along_z = lax.all_gather(rows, "zl", axis=0)
        order = [2 * zh, 2 * zh + 1, 2 - 2 * zh, 3 - 2 * zh]
        weights = [
            lax.all_gather(
                lax.dynamic_index_in_dim(along_z, m, 0, keepdims=False),
                ("y", "c"),
                axis=0,
                tiled=True,
            )
            for m in order
        ]
    with jax.named_scope("tokens"):
        far = lax.ppermute(tokens, "zh", [(0, 1), (1, 0)])
        chunks = ring_share(tokens, core) + ring_share(far, core)
    with jax.named_scope("direction"):
        vocab_rows = unembed.shape[0]
        dp_index = lax.axis_index(DP)
        ids = dp_index * vocab_rows + jnp.arange(vocab_rows, dtype=jnp.int32)
        one_hot = (clean[:, None] == ids[None, :]).astype(F32) - (
            corrupt[:, None] == ids[None, :]
        ).astype(F32)
        found = jnp.dot(one_hot.astype(BF16), unembed, preferred_element_type=F32)
        direction = jnp.sum(lax.all_to_all(found[:, None], DP, 0, 0, tiled=True), axis=0)
        weighted = final_gain.astype(F32) * direction[0]
        both = jnp.stack([weighted, tokens[LENGTH - 1].astype(F32)])
        wide = jnp.moveaxis(from_everyone(both, MP), 0, 1).reshape(2, 64, 128)
        columns = lax.all_to_all(jnp.moveaxis(wide, 1, 0), DP, 0, 0, tiled=True)
        weighted_cols, token_cols = (columns[:, 0], columns[:, 1])
        back_w = lax.dot_general(
            weighted_cols.astype(BF16), w_out, (((1,), (1,)), ((), ())), preferred_element_type=F32
        )
        grad_w = jnp.sum(lax.all_to_all(back_w[:, None], DP, 0, 0, tiled=True), axis=0)[0]
    with jax.named_scope("project"):
        acc, squares = (0.0, 0.0)
        for m, chunk, weight in zip(order, chunks, weights):
            t = chunk.astype(F32)
            g = lax.dynamic_slice_in_dim(gain, m * t.shape[1], t.shape[1], 0).astype(F32)
            squares = squares + jnp.sum(t * t, axis=1, keepdims=True)
            acc = acc + jnp.dot((t * g).astype(BF16), weight, preferred_element_type=F32)
        acc = acc * lax.rsqrt(squares / MODEL_WIDTH + 1e-05)
        heads = width // HEAD_SIZE
        acc = acc.reshape(2, LENGTH, heads + 2, HEAD_SIZE)
        cos, sin = rotary_tables()
        queries = rotate(acc[:, :, :heads], cos, sin).astype(BF16)
        keys = rotate(acc[:, :, heads : heads + 1], cos, sin)[:, :, 0].astype(BF16)
        values = acc[:, :, heads + 1].astype(BF16)
    with jax.named_scope("attend"):
        logits = jnp.einsum("btgd,bsd->bgts", queries, keys, preferred_element_type=F32)
        logits = logits / math.sqrt(HEAD_SIZE)
        causal = jnp.arange(LENGTH)[:, None] >= jnp.arange(LENGTH)[None, :]
        logits = jnp.where(causal, logits, -1e30)
        top = jnp.max(logits, axis=-1, keepdims=True)
        e = jnp.exp(logits - top)
        probs = (e / jnp.sum(e, axis=-1, keepdims=True)).astype(BF16)
        mixed = jnp.einsum("bgts,bsd->btgd", probs, values, preferred_element_type=F32)
        mixed = mixed.astype(BF16).reshape(2, LENGTH, width)
    with jax.named_scope("return_heads"):
        oa = send(mixed[0], lambda x, c: (x, x // 2) if c == 0 else (x + 2, x // 2))
        ob = send(mixed[1], lambda x, c: (x + 1, x // 2) if c == 0 else (x - 1, x // 2))
        head_out = jnp.concatenate(
            [jnp.where(odd == 0, oa, ob), jnp.where(odd == 0, ob, oa)], axis=1
        )
    with jax.named_scope("tail"):
        last = head_out[LENGTH - 1].astype(F32)
        total = jnp.sum(head_out.astype(F32), axis=0)
        every = from_everyone(jnp.stack([last, total]), DP)
        head_mean = jnp.sum(every[:, 1], axis=0) / TOKENS
        part = jnp.dot(every[:, 0].astype(BF16), w_out, preferred_element_type=F32)
        attn_last = jnp.sum(from_everyone(part, MP), axis=0).astype(BF16)
        residual = token_cols + attn_last.astype(F32)
        back_r = lax.dot_general(
            residual.astype(BF16), w_out, (((1,), (1,)), ((), ())), preferred_element_type=F32
        )
        sums = jnp.concatenate(
            [
                jnp.broadcast_to(jnp.sum(residual * residual, axis=1)[:, None], (64, 64)),
                jnp.broadcast_to(jnp.sum(residual * weighted_cols, axis=1)[:, None], (64, 64)),
            ],
            axis=1,
        )
        packed = jnp.concatenate([back_r, sums], axis=1)
        mine = jnp.sum(lax.all_to_all(packed[:, None], DP, 0, 0, tiled=True), axis=0)[0]
        grad_r, square, product = (mine[:1024], mine[1024], mine[1024 + 64])
        inverse = lax.rsqrt(square / MODEL_WIDTH + 1e-05)
        metric = inverse * product
        head_grads = grad_w * inverse - grad_r * (metric * inverse * inverse / MODEL_WIDTH)
        scores = jnp.sum(((head_mean - last) * head_grads).reshape(1, 8, HEAD_SIZE), axis=2)
    return (head_out, scores, metric[None])


def solution(mesh):
    fine = Mesh(mesh.devices.reshape(4, 4, 4, 2, 2), (*DP, *MP))
    in_specs = (
        P(DP, MP),
        P(),
        P(DP, MP),
        P(DP, MP),
        P(DP, MP),
        P(MP, DP),
        P(MP),
        P(DP, MP),
        P(),
        P(),
    )
    out_specs = (P(DP, MP), P(DP, MP), P(DP))
    return jax.shard_map(
        per_device, mesh=fine, in_specs=in_specs, out_specs=out_specs, check_vma=False
    )
```

profile of v0, /device:TPU:2, one launch (start us, length us, event | category | flops | bytes accessed | tf_op | source)
XLA Modules:
  0.0 342.4 jit_solution(12943895693049163494)
XLA Ops:
  9.7 2.4 collective-permute-start.4
  12.1 5.0 %collective-permute-done.4 = bf16[128,768]{1,0:T(8,128)(2,1)S(1)} collective-permute-done((bf16[128,768]{1,0:T(8,128)(2,1)S(1)}, bf16[128,768]{1,0:T(8,128)(2,1)S(1)}, u32[]{:S(2)}, u32[]{:S(2)}) %collective-permute-start.4) | collective-permute-done | bytes 196640 | tf_op jit(solution)/shard_map/weights/ppermute | solution.py:31
  18.0 47.1 %all-gather.11.cloned.1.call-done = bf16[1024,768]{1,0:T(8,128)(2,1)} async-done(((bf16[256,768]{1,0:T(8,128)(2,1)}), bf16[1024,768]{1,0:T(8,128)(2,1)}) %all-gather.11.cloned.1.call-update) | async-done | bytes 1572880 | tf_op jit(solution)/shard_map/weights/all_gather | solution.py:70
  65.1 2.5 constant_dynamic-slice_fusion
  69.0 3.9 %collective-permute-start.6 = (bf16[256,2048]{1,0:T(8,128)(2,1)S(1)}, bf16[256,2048]{1,0:T(8,128)(2,1)}, u32[]{:S(2)}, u32[]{:S(2)}) collective-permute-start(bf16[256,2048]{1,0:T(8,128)(2,1)S(1)} %copy-done.8), channel_id=1, source_target_pairs={{0,2},{2,0},{1,3},{3,1},{4,6},{6,4},{5,7},{7,5},{8,10},{10,8},{9,1... | collective-permute-start | bytes 3145736 | tf_op jit(solution)/shard_map/tokens/ppermute | solution.py:82
  76.1 3.1 convolution_bitcast_fusion
  80.5 9.1 %all-to-all-start.1 = ((f32[64,1,2048]{2,1,0:T(1,128)}), f32[64,1,2048]{2,1,0:T(1,128)S(1)}, u32[]{:S(2)}, u32[]{:S(2)}) async-start(f32[64,1,2048]{2,1,0:T(1,128)} %copy.55), calls=%async_computation.1 | async-start | bytes 1048576 | tf_op jit(solution)/shard_map/direction/all_to_all | solution.py:92
  90.1 2.3 collective-permute-start.2
  94.9 39.4 %all-to-all-done.1 = f32[64,1,2048]{2,1,0:T(1,128)S(1)} async-done(((f32[64,1,2048]{2,1,0:T(1,128)}), f32[64,1,2048]{2,1,0:T(1,128)S(1)}, u32[]{:S(2)}, u32[]{:S(2)}) %all-to-all-start.1) | async-done | bytes 524320 | tf_op jit(solution)/shard_map/direction/all_to_all | solution.py:92
  136.8 3.0 collective-permute-start.9
  145.3 35.7 %collective-permute-done.8 = bf16[256,2048]{1,0:T(8,128)(2,1)S(1)} collective-permute-done((bf16[256,2048]{1,0:T(8,128)(2,1)}, bf16[256,2048]{1,0:T(8,128)(2,1)S(1)}, u32[]{:S(2)}, u32[]{:S(2)}) %collective-permute-start.8) | collective-permute-done | bytes 1048608 | tf_op jit(solution)/shard_map/tokens/ppermute | solution.py:31
  181.0 3.1 collective-permute-done.9
  188.0 5.6 %fusion.11 = f32[512,768]{1,0:T(8,128)} fusion(bf16[1,2048,768]{2,1,0:T(8,128)(2,1)} %all-gather.17.cloned.1.call-done, f32[2048]{0:T(1024)} %get-tuple-element.42, bf16[256,2048]{1,0:T(8,128)(2,1)} %copy-done.1, bf16[256,2048]{1,0:T(8,128)(2,1)} %copy-done.6), kind=kOutput, calls=%fused_computation.19 | convolution fusion | flops 1616904192 | bytes 6823936 | tf_op jit(solution)/shard_map/project/dot_general | solution.py:108
  193.6 5.2 %fusion.13 = f32[512,768]{1,0:T(8,128)} fusion(bf16[1,2048,768]{2,1,0:T(8,128)(2,1)} %all-gather.15.cloned.1.call-done, f32[2048]{0:T(1024)} %get-tuple-element.40, bf16[256,2048]{1,0:T(8,128)(2,1)S(1)} %get-tuple-element.11, bf16[256,2048]{1,0:T(8,128)(2,1)} %copy-done.3), kind=kOutput, calls=%fused_computation.21 | convolution fusion | flops 1616904192 | bytes 6823936 | tf_op jit(solution)/shard_map/project/dot_general | solution.py:108
  198.8 5.3 %fusion.15 = f32[512,768]{1,0:T(8,128)} fusion(bf16[1,2048,768]{2,1,0:T(8,128)(2,1)} %all-gather.13.cloned.1.call-done, f32[2048]{0:T(1024)} %get-tuple-element.41, bf16[256,2048]{1,0:T(8,128)(2,1)S(1)} %get-tuple-element.12, bf16[256,2048]{1,0:T(8,128)(2,1)} %copy-done.2), kind=kOutput, calls=%fused_computation.23 | convolution fusion | flops 1616904192 | bytes 6823936 | tf_op jit(solution)/shard_map/project/dot_general | solution.py:108
  204.1 6.3 %add_multiply_fusion = f32[512,768]{1,0:T(8,128)} fusion(f32[512,768]{1,0:T(8,128)} %fusion.11, f32[512,768]{1,0:T(8,128)} %fusion.15, f32[512,768]{1,0:T(8,128)} %fusion.13, bf16[1,2048,768]{2,1,0:T(8,128)(2,1)} %all-gather.19.cloned.1.call-done, f32[2048]{0:T(1024)} %get-tuple-element.39, bf16[256,2048]{1,0:T(8,128)(2,1)S(1)} %get-tuple-element.9, ...), kind=kOutput, calls=%fused_computation.38 | convolution fusion | flops 1618477056 | bytes 11544576 | tf_op jit(solution)/shard_map/project/dot_general | solution.py:108
  220.4 3.5 %fusion.75 = (f32[2,4,256]{2,1,0:T(4,128)S(1)}, f32[2,4,256,256]{2,3,1,0:T(8,128)}) fusion(pred[256,256]{0,1:T(8,128)(4,1)} %iota_compare_fusion, bf16[2,256,4,64]{3,1,2,0:T(8,128)(2,1)} %get-tuple-element.8, bf16[2,256,4,64]{3,1,2,0:T(8,128)(2,1)S(1)} %get-tuple-element.7, bf16[2,256,1,64]{3,1,0,2:T(8,128)(2,1)S(1)} %copy-done.10, ...), kind=kOutput, calls=%fused_computation.132 | convolution fusion | flops 137625856 | bytes 2826240 | tf_op jit(solution)/shard_map/attend/sub | solution.py:122
  223.9 1.9 fusion.30
  226.8 2.7 collective-permute-start.12
  230.2 3.3 all-to-all-start.2
  233.5 2.7 collective-permute-done.12
  237.2 4.9 %all-to-all-done.2 = f32[4,2,2048]{2,1,0:T(2,128)S(1)} async-done(((f32[4,2,2048]{2,1,0:T(2,128)}), f32[4,2,2048]{2,1,0:T(2,128)S(1)}, u32[]{:S(2)}, u32[]{:S(2)}) %all-to-all-start.2) | async-done | bytes 65568 | tf_op jit(solution)/shard_map/direction/all_to_all | solution.py:19
  243.1 8.4 %all-to-all-start = ((f32[64,2,1024]{2,1,0:T(2,128)}), f32[64,2,1024]{2,1,0:T(2,128)S(1)}, u32[]{:S(2)}, u32[]{:S(2)}) async-start(f32[64,2,1024]{2,1,0:T(2,128)} %broadcast_in_dim.26), calls=%async_computation | async-start | bytes 1048576 | tf_op jit(solution)/shard_map/tail/all_to_all | solution.py:19
  252.3 16.1 %all-to-all-done = f32[64,2,1024]{2,1,0:T(2,128)S(1)} async-done(((f32[64,2,1024]{2,1,0:T(2,128)}), f32[64,2,1024]{2,1,0:T(2,128)S(1)}, u32[]{:S(2)}, u32[]{:S(2)}) %all-to-all-start) | async-done | bytes 524320 | tf_op jit(solution)/shard_map/tail/all_to_all | solution.py:19
  268.3 5.9 %all-to-all-start.3 = ((f32[64,2,128]{2,1,0:T(2,128)}), f32[64,2,128]{2,1,0:T(2,128)S(1)}, u32[]{:S(2)}, u32[]{:S(2)}) async-start(f32[64,2,128]{2,1,0:T(2,128)} %copy.57), calls=%async_computation.3 | async-start | bytes 131072 | tf_op jit(solution)/shard_map/direction/all_to_all | solution.py:96
  274.6 8.9 %all-to-all-done.3 = f32[64,2,128]{2,1,0:T(2,128)S(1)} async-done(((f32[64,2,128]{2,1,0:T(2,128)}), f32[64,2,128]{2,1,0:T(2,128)S(1)}, u32[]{:S(2)}, u32[]{:S(2)}) %all-to-all-start.3) | async-done | bytes 65568 | tf_op jit(solution)/shard_map/direction/all_to_all | solution.py:96
  284.2 3.3 all-to-all-start.5
  288.8 7.3 %all-to-all-done.5 = f32[4,64,128]{2,1,0:T(8,128)S(1)} async-done(((f32[4,64,128]{2,1,0:T(8,128)}), f32[4,64,128]{2,1,0:T(8,128)S(1)}, u32[]{:S(2)}, u32[]{:S(2)}) %all-to-all-start.5) | async-done | bytes 131104 | tf_op jit(solution)/shard_map/tail/all_to_all | solution.py:19
  296.0 6.4 %all-to-all-start.4 = ((f32[64,1,1024]{2,1,0:T(1,128)}), f32[64,1,1024]{2,1,0:T(1,128)S(1)}, u32[]{:S(2)}, u32[]{:S(2)}) async-start(f32[64,1,1024]{2,1,0:T(1,128)} %copy.59), calls=%async_computation.4 | async-start | bytes 524288 | tf_op jit(solution)/shard_map/direction/all_to_all | solution.py:101
  304.0 10.1 %all-to-all-done.4 = f32[64,1,1024]{2,1,0:T(1,128)S(1)} async-done(((f32[64,1,1024]{2,1,0:T(1,128)}), f32[64,1,1024]{2,1,0:T(1,128)S(1)}, u32[]{:S(2)}, u32[]{:S(2)}) %all-to-all-start.4) | async-done | bytes 262176 | tf_op jit(solution)/shard_map/direction/all_to_all | solution.py:101
  314.1 6.0 %all-to-all-start.6 = ((f32[64,1,1152]{2,1,0:T(1,128)}), f32[64,1,1152]{2,1,0:T(1,128)S(1)}, u32[]{:S(2)}, u32[]{:S(2)}) async-start(f32[64,1,1152]{2,1,0:T(1,128)} %copy.62), calls=%async_computation.6 | async-start | bytes 589824 | tf_op jit(solution)/shard_map/tail/all_to_all | solution.py:151
  320.7 11.3 %all-to-all-done.6 = f32[64,1,1152]{2,1,0:T(1,128)S(1)} async-done(((f32[64,1,1152]{2,1,0:T(1,128)}), f32[64,1,1152]{2,1,0:T(1,128)S(1)}, u32[]{:S(2)}, u32[]{:S(2)}) %all-to-all-start.6) | async-done | bytes 294944 | tf_op jit(solution)/shard_map/tail/all_to_all | solution.py:151
  (125 shorter events, 44.0 us)
Async XLA Ops:
  7.2 267.3 %copy-start = (bf16[1024,128]{1,0:T(8,128)(2,1)S(1)}, bf16[1024,128]{1,0:T(8,128)(2,1)}, u32[]{:S(2)}) copy-start(bf16[1024,128]{1,0:T(8,128)(2,1)} %param.15) | copy-start | bytes 786436
  7.2 57.9 %all-gather.11.cloned.1.call-start = ((), (), s32[]{:S(2)}) async-start(), calls=%async_computation.7 | async-start | bytes 1966080 | tf_op jit(solution)/shard_map/weights/all_gather | solution.py:70
  9.1 3.0 collective-permute-start.3
  9.7 7.3 %collective-permute-start.4 = (bf16[128,768]{1,0:T(8,128)(2,1)S(1)}, bf16[128,768]{1,0:T(8,128)(2,1)S(1)}, u32[]{:S(2)}, u32[]{:S(2)}) collective-permute-start(bf16[128,768]{1,0:T(8,128)(2,1)S(1)} %get-tuple-element.38), channel_id=1, source_target_pairs={{0,4},{1,12},{4,0},{5,8},{8,5},{9,13},{12,1},{13,9},{2,6},{3,14},{... | collective-permute-start | bytes 589832 | tf_op jit(solution)/shard_map/weights/ppermute | solution.py:31
  12.1 56.9 %copy-start.8 = (bf16[256,2048]{1,0:T(8,128)(2,1)S(1)}, bf16[256,2048]{1,0:T(8,128)(2,1)}, u32[]{:S(2)}) copy-start(bf16[256,2048]{1,0:T(8,128)(2,1)} %param.10) | copy-start | bytes 3145732
  17.1 58.9 %copy-start.13 = (s32[64]{0:T(128)S(1)}, s32[64]{0:T(128)}, u32[]{:S(2)}) copy-start(s32[64]{0:T(128)} %param.19) | copy-start | bytes 772
  17.1 58.9 %copy-start.14 = (s32[64]{0:T(128)S(1)}, s32[64]{0:T(128)}, u32[]{:S(2)}) copy-start(s32[64]{0:T(128)} %param.18) | copy-start | bytes 772
  17.9 170.1 %all-gather.17.cloned.1.call-start = ((), (), s32[]{:S(2)}) async-start(), calls=%async_computation.10 | async-start | bytes 3538944 | tf_op jit(solution)/shard_map/weights/all_gather | solution.py:73
  67.6 126.0 %all-gather.15.cloned.1.call-start = ((), (), s32[]{:S(2)}) async-start(), calls=%async_computation.9 | async-start | bytes 3538944 | tf_op jit(solution)/shard_map/weights/all_gather | solution.py:73
  68.4 130.5 %all-gather.13.cloned.1.call-start = ((), (), s32[]{:S(2)}) async-start(), calls=%async_computation.8 | async-start | bytes 3538944 | tf_op jit(solution)/shard_map/weights/all_gather | solution.py:73
  68.9 135.2 %all-gather.19.cloned.1.call-start = ((), (), s32[]{:S(2)}) async-start(), calls=%async_computation.11 | async-start | bytes 3538944 | tf_op jit(solution)/shard_map/weights/all_gather | solution.py:73
  69.0 65.6 %collective-permute-start.6 = (bf16[256,2048]{1,0:T(8,128)(2,1)S(1)}, bf16[256,2048]{1,0:T(8,128)(2,1)}, u32[]{:S(2)}, u32[]{:S(2)}) collective-permute-start(bf16[256,2048]{1,0:T(8,128)(2,1)S(1)} %copy-done.8), channel_id=1, source_target_pairs={{0,2},{2,0},{1,3},{3,1},{4,6},{6,4},{5,7},{7,5},{8,10},{10,8},{9,1... | collective-permute-start | bytes 3145736 | tf_op jit(solution)/shard_map/tokens/ppermute | solution.py:82
  72.9 62.4 %collective-permute-start = (bf16[256,2048]{1,0:T(8,128)(2,1)S(1)}, bf16[256,2048]{1,0:T(8,128)(2,1)}, u32[]{:S(2)}, u32[]{:S(2)}) collective-permute-start(bf16[256,2048]{1,0:T(8,128)(2,1)S(1)} %copy-done.8), channel_id=1, source_target_pairs={{0,9},{1,0},{4,13},{5,4},{8,1},{9,8},{12,5},{13,12},{2,11},{3,2},{... | collective-permute-start | bytes 3145736 | tf_op jit(solution)/shard_map/tokens/ppermute | solution.py:31
  74.4 62.4 %collective-permute-start.5 = (bf16[256,2048]{1,0:T(8,128)(2,1)S(1)}, bf16[256,2048]{1,0:T(8,128)(2,1)}, u32[]{:S(2)}, u32[]{:S(2)}) collective-permute-start(bf16[256,2048]{1,0:T(8,128)(2,1)S(1)} %copy-done.8), channel_id=1, source_target_pairs={{1,9},{5,13},{9,1},{13,5},{3,11},{7,15},{11,3},{15,7},{17,25},{21,... | collective-permute-start | bytes 3145736 | tf_op jit(solution)/shard_map/tokens/ppermute | solution.py:31
  76.1 18.2 %copy-start.11 = (bf16[8192]{0:T(1024)(128)(2,1)S(1)}, bf16[8192]{0:T(1024)(128)(2,1)}, u32[]{:S(2)}) copy-start(bf16[8192]{0:T(1024)(128)(2,1)} %param.11) | copy-start | bytes 49156
  80.5 53.8 %all-to-all-start.1 = ((f32[64,1,2048]{2,1,0:T(1,128)}), f32[64,1,2048]{2,1,0:T(1,128)S(1)}, u32[]{:S(2)}, u32[]{:S(2)}) async-start(f32[64,1,2048]{2,1,0:T(1,128)} %copy.55), calls=%async_computation.1 | async-start | bytes 1048576 | tf_op jit(solution)/shard_map/direction/all_to_all | solution.py:92
  89.6 51.6 %collective-permute-start.1 = (bf16[256,2048]{1,0:T(8,128)(2,1)S(1)}, bf16[256,2048]{1,0:T(8,128)(2,1)S(1)}, u32[]{:S(2)}, u32[]{:S(2)}) collective-permute-start(bf16[256,2048]{1,0:T(8,128)(2,1)S(1)} %copy-done.8), channel_id=1, source_target_pairs={{0,12},{1,5},{4,0},{5,9},{8,4},{9,13},{12,8},{13,1},{2,14},{3,7},{... | collective-permute-start | bytes 3145736 | tf_op jit(solution)/shard_map/tokens/ppermute | solution.py:31
  90.1 52.8 %collective-permute-start.2 = (bf16[256,2048]{1,0:T(8,128)(2,1)S(1)}, bf16[256,2048]{1,0:T(8,128)(2,1)}, u32[]{:S(2)}, u32[]{:S(2)}) collective-permute-start(bf16[256,2048]{1,0:T(8,128)(2,1)S(1)} %copy-done.8), channel_id=1, source_target_pairs={{0,5},{1,12},{4,9},{5,0},{8,13},{9,4},{12,1},{13,8},{2,7},{3,14},{... | collective-permute-start | bytes 3145736 | tf_op jit(solution)/shard_map/tokens/ppermute | solution.py:31
  134.6 49.7 %collective-permute-start.10 = (bf16[256,2048]{1,0:T(8,128)(2,1)}, bf16[256,2048]{1,0:T(8,128)(2,1)S(1)}, u32[]{:S(2)}, u32[]{:S(2)}) collective-permute-start(bf16[256,2048]{1,0:T(8,128)(2,1)} %collective-permute-done.6), channel_id=1, source_target_pairs={{1,9},{5,13},{9,1},{13,5},{3,11},{7,15},{11,3},{15,7},{17,25},{21,... | collective-permute-start | bytes 3145736 | tf_op jit(solution)/shard_map/tokens/ppermute | solution.py:31
  135.3 45.7 %collective-permute-start.8 = (bf16[256,2048]{1,0:T(8,128)(2,1)}, bf16[256,2048]{1,0:T(8,128)(2,1)S(1)}, u32[]{:S(2)}, u32[]{:S(2)}) collective-permute-start(bf16[256,2048]{1,0:T(8,128)(2,1)} %collective-permute-done.6), channel_id=1, source_target_pairs={{0,12},{1,5},{4,0},{5,9},{8,4},{9,13},{12,8},{13,1},{2,14},{3,7},{... | collective-permute-start | bytes 3145736 | tf_op jit(solution)/shard_map/tokens/ppermute | solution.py:31
  136.8 47.3 %collective-permute-start.9 = (bf16[256,2048]{1,0:T(8,128)(2,1)}, bf16[256,2048]{1,0:T(8,128)(2,1)S(1)}, u32[]{:S(2)}, u32[]{:S(2)}) collective-permute-start(bf16[256,2048]{1,0:T(8,128)(2,1)} %collective-permute-done.6), channel_id=1, source_target_pairs={{0,5},{1,12},{4,9},{5,0},{8,13},{9,4},{12,1},{13,8},{2,7},{3,14},{... | collective-permute-start | bytes 3145736 | tf_op jit(solution)/shard_map/tokens/ppermute | solution.py:31
  141.2 43.1 %collective-permute-start.7 = (bf16[256,2048]{1,0:T(8,128)(2,1)}, bf16[256,2048]{1,0:T(8,128)(2,1)S(1)}, u32[]{:S(2)}, u32[]{:S(2)}) collective-permute-start(bf16[256,2048]{1,0:T(8,128)(2,1)} %collective-permute-done.6), channel_id=1, source_target_pairs={{0,9},{1,0},{4,13},{5,4},{8,1},{9,8},{12,5},{13,12},{2,11},{3,2},{... | collective-permute-start | bytes 3145736 | tf_op jit(solution)/shard_map/tokens/ppermute | solution.py:31
  198.8 5.3 %copy-start.5 = (bf16[256,2048]{1,0:T(8,128)(2,1)S(1)}, bf16[256,2048]{1,0:T(8,128)(2,1)}, u32[]{:S(2)}) copy-start(bf16[256,2048]{1,0:T(8,128)(2,1)} %copy-done.4) | copy-start | bytes 3145732
  223.9 5.7 %copy-start.12 = (bf16[2048]{0:T(1024)(128)(2,1)S(1)}, bf16[2048]{0:T(1024)(128)(2,1)}, u32[]{:S(2)}) copy-start(bf16[2048]{0:T(1024)(128)(2,1)} %param.16) | copy-start | bytes 12292
  226.0 7.5 %collective-permute-start.11 = (bf16[256,512]{1,0:T(8,128)(2,1)S(1)}, bf16[256,512]{1,0:T(8,128)(2,1)S(1)}, u32[]{:S(2)}, u32[]{:S(2)}) collective-permute-start(bf16[256,512]{1,0:T(8,128)(2,1)S(1)} %copy.53), channel_id=1, source_target_pairs={{0,0},{1,8},{4,4},{5,12},{8,9},{9,1},{12,13},{13,5},{2,2},{3,10},{... | collective-permute-start | bytes 786440 | tf_op jit(solution)/shard_map/return_heads/ppermute | solution.py:31
  226.8 9.4 %collective-permute-start.12 = (bf16[256,512]{1,0:T(8,128)(2,1)S(1)}, bf16[256,512]{1,0:T(8,128)(2,1)S(1)}, u32[]{:S(2)}, u32[]{:S(2)}) collective-permute-start(bf16[256,512]{1,0:T(8,128)(2,1)S(1)} %copy.54), channel_id=1, source_target_pairs={{0,4},{1,12},{4,8},{5,0},{8,13},{9,5},{12,1},{13,9},{2,6},{3,14},{... | collective-permute-start | bytes 786440 | tf_op jit(solution)/shard_map/return_heads/ppermute | solution.py:31
  230.2 11.9 %all-to-all-start.2 = ((f32[4,2,2048]{2,1,0:T(2,128)}), f32[4,2,2048]{2,1,0:T(2,128)S(1)}, u32[]{:S(2)}, u32[]{:S(2)}) async-start(f32[4,2,2048]{2,1,0:T(2,128)} %broadcast_in_dim.28), calls=%async_computation.2 | async-start | bytes 131072 | tf_op jit(solution)/shard_map/direction/all_to_all | solution.py:19
  243.1 25.3 %all-to-all-start = ((f32[64,2,1024]{2,1,0:T(2,128)}), f32[64,2,1024]{2,1,0:T(2,128)S(1)}, u32[]{:S(2)}, u32[]{:S(2)}) async-start(f32[64,2,1024]{2,1,0:T(2,128)} %broadcast_in_dim.26), calls=%async_computation | async-start | bytes 1048576 | tf_op jit(solution)/shard_map/tail/all_to_all | solution.py:19
  268.3 15.2 %all-to-all-start.3 = ((f32[64,2,128]{2,1,0:T(2,128)}), f32[64,2,128]{2,1,0:T(2,128)S(1)}, u32[]{:S(2)}, u32[]{:S(2)}) async-start(f32[64,2,128]{2,1,0:T(2,128)} %copy.57), calls=%async_computation.3 | async-start | bytes 131072 | tf_op jit(solution)/shard_map/direction/all_to_all | solution.py:96
  284.2 11.8 %all-to-all-start.5 = ((f32[4,64,128]{2,1,0:T(8,128)}), f32[4,64,128]{2,1,0:T(8,128)S(1)}, u32[]{:S(2)}, u32[]{:S(2)}) async-start(f32[4,64,128]{2,1,0:T(8,128)} %broadcast_in_dim.30), calls=%async_computation.5 | async-start | bytes 262144 | tf_op jit(solution)/shard_map/tail/all_to_all | solution.py:19
  296.0 18.1 %all-to-all-start.4 = ((f32[64,1,1024]{2,1,0:T(1,128)}), f32[64,1,1024]{2,1,0:T(1,128)S(1)}, u32[]{:S(2)}, u32[]{:S(2)}) async-start(f32[64,1,1024]{2,1,0:T(1,128)} %copy.59), calls=%async_computation.4 | async-start | bytes 524288 | tf_op jit(solution)/shard_map/direction/all_to_all | solution.py:101
  314.1 17.8 %all-to-all-start.6 = ((f32[64,1,1152]{2,1,0:T(1,128)}), f32[64,1,1152]{2,1,0:T(1,128)S(1)}, u32[]{:S(2)}, u32[]{:S(2)}) async-start(f32[64,1,1152]{2,1,0:T(1,128)} %copy.62), calls=%async_computation.6 | async-start | bytes 589824 | tf_op jit(solution)/shard_map/tail/all_to_all | solution.py:151
  (8 other events, 21.6 us)
Sparse Core Ops, SparseCore 0:
  18.0 46.9 all-gather.10
  67.7 30.0 all-gather.16
  99.7 34.6 all-gather.14
  136.1 30.1 all-gather.12
  168.0 30.3 all-gather.18
where the time goes:
time: 344 us; the launch traced here: 342 us
  waiting for transfers between devices  193 us (56%)
  starting transfers between devices  65.8 us (19%)
  matrix products  31.4 us (9%)
  local copies, waits for them, and re-layouts  18.8 us (5%)
  other arithmetic  16.8 us (5%)
  between operations  16.8 us (5%)
    all_gather x1, waiting for transfers between devices, per_device(): along_z = lax.all_gather(rows, 'zl', axis=0)  47.1 us
    ppermute x12, waiting for transfers between devices, send(): return lax.ppermute(value, ('x', 'c'), pairs)  46.6 us
    all_to_all x1, waiting for transfers between devices, per_device(): lax.all_to_all(found[:, None], DP, 0, 0, tiled=True)  39.4 us
    all_to_all x3, waiting for transfers between devices, from_everyone(): lax.all_to_all(jnp.broadcast_to(value[None], (count, *value.shape)), axis...  28.3 us
    dot_general x4, matrix products, per_device(): jnp.dot((t * g).astype(BF16), weight, preferred_element_type=F32)  22.3 us
    ppermute x12, starting transfers between devices, send(): return lax.ppermute(value, ('x', 'c'), pairs)  19.2 us
    all_to_all x3, starting transfers between devices, from_everyone(): lax.all_to_all(jnp.broadcast_to(value[None], (count, *value.shape)), axis...  15 us
    all_to_all x1, waiting for transfers between devices, per_device(): lax.all_to_all(packed[:, None], DP, 0, 0, tiled=True)  11.3 us
  transfers between devices with their start and end apart: 25, of which 12 were waited for; matrix products, arithmetic and copies ran while one was open for 11% of the time, Pallas kernels for 0%

commit v1 on v0

--- a/solution.py
+++ b/solution.py
@@ -70,11 +70,17 @@
         along_z = lax.all_gather(rows, "zl", axis=0)
         order = [2 * zh, 2 * zh + 1, 2 - 2 * zh, 3 - 2 * zh]
         weights = [
-            lax.all_gather(
-                lax.dynamic_index_in_dim(along_z, m, 0, keepdims=False),
-                ("y", "c"),
+            jnp.concatenate(
+                lax.all_to_all(
+                    jnp.stack(
+                        [lax.dynamic_index_in_dim(along_z, m, 0, keepdims=False)]
+                        * lax.axis_size(("y", "c"))
+                    ),
+                    ("y", "c"),
+                    0,
+                    0,
+                ),
                 axis=0,
-                tiled=True,
             )
             for m in order
         ]

time: 344 us -> 428 us (1.24)
  blocking collectives: 0 us -> 85.3 us
  waiting for transfers between devices: 193 us -> 170 us
  starting transfers between devices: 65.8 us -> 87 us
  matrix products: 31.4 us -> 26.3 us
    all_to_all x0 -> x2, blocking collectives: none -> 85.3 us  [per_device(): lax.all_to_all(jnp.stack([lax.dynamic_index_in_dim(along_z, m, 0, keepdim...]
    all_to_all x1, waiting for transfers between devices: 39.4 us -> 0.01 us  [per_device(): lax.all_to_all(found[:, None], DP, 0, 0, tiled=True)]
    ppermute x1, waiting for transfers between devices: 0.01 us -> 16.8 us  [per_device(): far = lax.ppermute(tokens, 'zh', [(0, 1), (1, 0)])]
    all_gather x1, waiting for transfers between devices: 47.1 us -> 35.9 us  [per_device(): along_z = lax.all_gather(rows, 'zl', axis=0)]
    ppermute x12, waiting for transfers between devices: 46.6 us -> 56.5 us  [send(): return lax.ppermute(value, ('x', 'c'), pairs)]
    all_to_all x3, starting transfers between devices: 15 us -> 24.9 us  [from_everyone(): lax.all_to_all(jnp.broadcast_to(value[None], (count, *value.shape)), axis...]
    all_to_all x0 -> x2, starting transfers between devices: none -> 9.2 us  [per_device(): lax.all_to_all(jnp.stack([lax.dynamic_index_in_dim(along_z, m, 0, keepdim...]
    all_to_all x1, starting transfers between devices: 9.1 us -> 14.4 us  [per_device(): lax.all_to_all(found[:, None], DP, 0, 0, tiled=True)]
  transfers between devices with their start and end apart: 25 -> 23, of which waited for: 12 -> 12; matrix products, arithmetic and copies ran while one was open for 11% -> 9% of each run, Pallas kernels for 0% -> 0%
where the time goes in v1:
time: 428 us; the launch traced here: 427 us
  waiting for transfers between devices  170 us (40%)
  starting transfers between devices  87 us (20%)
  blocking collectives  85.3 us (20%)
  matrix products  26.3 us (6%)
  local copies, waits for them, and re-layouts  22.2 us (5%)
  other arithmetic  19.2 us (4%)
  between operations  17.1 us (4%)
    all_to_all x2, blocking collectives, per_device(): lax.all_to_all(jnp.stack([lax.dynamic_index_in_dim(along_z, m, 0, keepdim...  85.3 us
    ppermute x12, waiting for transfers between devices, send(): return lax.ppermute(value, ('x', 'c'), pairs)  56.5 us
    all_gather x1, waiting for transfers between devices, per_device(): along_z = lax.all_gather(rows, 'zl', axis=0)  35.9 us
    all_to_all x3, waiting for transfers between devices, from_everyone(): lax.all_to_all(jnp.broadcast_to(value[None], (count, *value.shape)), axis...  30.4 us
    all_to_all x3, starting transfers between devices, from_everyone(): lax.all_to_all(jnp.broadcast_to(value[None], (count, *value.shape)), axis...  24.9 us
    dot_general x4, matrix products, per_device(): jnp.dot((t * g).astype(BF16), weight, preferred_element_type=F32)  17.2 us
    ppermute x1, waiting for transfers between devices, per_device(): far = lax.ppermute(tokens, 'zh', [(0, 1), (1, 0)])  16.8 us
    ppermute x12, starting transfers between devices, send(): return lax.ppermute(value, ('x', 'c'), pairs)  15.6 us
  transfers between devices with their start and end apart: 23, of which 12 were waited for; matrix products, arithmetic and copies ran while one was open for 9% of the time, Pallas kernels for 0%

profile of v1, /device:TPU:2, one launch (start us, length us, event | category | flops | bytes accessed | tf_op | source)
XLA Modules:
  0.0 427.0 jit_solution(17555884296295741904)
XLA Ops:
  9.8 2.4 collective-permute-start.4
  12.1 5.0 %collective-permute-done.4 = bf16[128,768]{1,0:T(8,128)(2,1)S(1)} collective-permute-done((bf16[128,768]{1,0:T(8,128)(2,1)S(1)}, bf16[128,768]{1,0:T(8,128)(2,1)S(1)}, u32[]{:S(2)}, u32[]{:S(2)}) %collective-permute-start.4) | collective-permute-done | bytes 196640 | tf_op jit(solution)/shard_map/weights/ppermute | solution.py:31
  18.0 3.1 convolution_bitcast_fusion
  22.4 14.4 %all-to-all-start.5 = ((f32[64,1,2048]{2,1,0:T(1,128)}), f32[64,1,2048]{2,1,0:T(1,128)S(1)}, u32[]{:S(2)}, u32[]{:S(2)}) async-start(f32[64,1,2048]{2,1,0:T(1,128)} %copy.55), calls=%async_computation.5 | async-start | bytes 1048576 | tf_op jit(solution)/shard_map/direction/all_to_all | solution.py:98
  36.8 35.9 %all-gather.3.cloned.1.call-done = bf16[1024,768]{1,0:T(8,128)(2,1)} async-done(((bf16[256,768]{1,0:T(8,128)(2,1)}), bf16[1024,768]{1,0:T(8,128)(2,1)}) %all-gather.3.cloned.1.call-update) | async-done | bytes 1572880 | tf_op jit(solution)/shard_map/weights/all_gather | solution.py:70
  74.4 43.1 %all_to_all.55 = bf16[8,256,768]{2,1,0:T(8,128)(2,1)} all-to-all(bf16[8,256,768]{2,1,0:T(8,128)(2,1)S(1)} %stack.18), channel_id=1, replica_groups=mesh['zl'=4,'y'=4,'x'=4,'zh'=2,'c'=2] {'y','c'}, dimensions={0} | all-to-all | bytes 6291456 | tf_op jit(solution)/shard_map/weights/all_to_all | solution.py:74
  117.7 42.1 %all_to_all.56 = bf16[8,256,768]{2,1,0:T(8,128)(2,1)} all-to-all(bf16[8,256,768]{2,1,0:T(8,128)(2,1)S(1)} %stack.17), channel_id=1, replica_groups=mesh['zl'=4,'y'=4,'x'=4,'zh'=2,'c'=2] {'y','c'}, dimensions={0} | all-to-all | bytes 6291456 | tf_op jit(solution)/shard_map/weights/all_to_all | solution.py:74
  161.7 4.6 %all-to-all-start = ((bf16[8,256,768]{2,1,0:T(8,128)(2,1)}), bf16[8,256,768]{2,1,0:T(8,128)(2,1)}, u32[]{:S(2)}, u32[]{:S(2)}) async-start(bf16[8,256,768]{2,1,0:T(8,128)(2,1)} %stack.16), calls=%async_computation | async-start | bytes 6291456 | tf_op jit(solution)/shard_map/weights/all_to_all | solution.py:74
  166.3 4.6 %collective-permute-start.6 = (bf16[256,2048]{1,0:T(8,128)(2,1)S(1)}, bf16[256,2048]{1,0:T(8,128)(2,1)}, u32[]{:S(2)}, u32[]{:S(2)}) collective-permute-start(bf16[256,2048]{1,0:T(8,128)(2,1)S(1)} %copy-done.10), channel_id=1, source_target_pairs={{0,2},{2,0},{1,3},{3,1},{4,6},{6,4},{5,7},{7,5},{8,10},{10,8},{9,1... | collective-permute-start | bytes 3145736 | tf_op jit(solution)/shard_map/tokens/ppermute | solution.py:88
  172.6 3.2 collective-permute-start
  179.3 16.8 %collective-permute-done.6 = bf16[256,2048]{1,0:T(8,128)(2,1)} collective-permute-done((bf16[256,2048]{1,0:T(8,128)(2,1)S(1)}, bf16[256,2048]{1,0:T(8,128)(2,1)}, u32[]{:S(2)}, u32[]{:S(2)}) %collective-permute-start.6) | collective-permute-done | bytes 1048608 | tf_op jit(solution)/shard_map/tokens/ppermute | solution.py:88
  197.7 2.1 collective-permute-start.9
  202.3 22.0 %collective-permute-done.2 = bf16[256,2048]{1,0:T(8,128)(2,1)} collective-permute-done((bf16[256,2048]{1,0:T(8,128)(2,1)S(1)}, bf16[256,2048]{1,0:T(8,128)(2,1)}, u32[]{:S(2)}, u32[]{:S(2)}) %collective-permute-start.2) | collective-permute-done | bytes 1048608 | tf_op jit(solution)/shard_map/tokens/ppermute | solution.py:31
  230.3 4.6 %all-to-all-start.3 = ((bf16[8,256,768]{2,1,0:T(8,128)(2,1)}), bf16[8,256,768]{2,1,0:T(8,128)(2,1)}, u32[]{:S(2)}, u32[]{:S(2)}) async-start(bf16[8,256,768]{2,1,0:T(8,128)(2,1)} %stack.19), calls=%async_computation.3 | async-start | bytes 6291456 | tf_op jit(solution)/shard_map/weights/all_to_all | solution.py:74
  234.9 29.3 %collective-permute-done.9 = bf16[256,2048]{1,0:T(8,128)(2,1)} collective-permute-done((bf16[256,2048]{1,0:T(8,128)(2,1)}, bf16[256,2048]{1,0:T(8,128)(2,1)}, u32[]{:S(2)}, u32[]{:S(2)}) %collective-permute-start.9) | collective-permute-done | bytes 1048608 | tf_op jit(solution)/shard_map/tokens/ppermute | solution.py:31
  270.1 3.0 fusion.11
  273.1 3.0 fusion.13
  276.1 5.0 %fusion.15 = f32[512,768]{1,0:T(8,128)} fusion(bf16[2048,768]{1,0:T(8,128)(2,1)} %bitcast.2, f32[2048]{0:T(1024)S(1)} %copy-done.16, bf16[256,2048]{1,0:T(8,128)(2,1)S(1)} %get-tuple-element.12, bf16[256,2048]{1,0:T(8,128)(2,1)S(1)} %copy-done.2), kind=kOutput, calls=%fused_computation.21 | convolution fusion | flops 1616904192 | bytes 6823936 | tf_op jit(solution)/shard_map/project/dot_general | solution.py:114
  281.1 6.3 %add_multiply_fusion = f32[512,768]{1,0:T(8,128)} fusion(f32[512,768]{1,0:T(8,128)} %fusion.11, f32[512,768]{1,0:T(8,128)} %fusion.15, f32[512,768]{1,0:T(8,128)} %fusion.13, bf16[2048,768]{1,0:T(8,128)(2,1)} %bitcast.8, f32[2048]{0:T(1024)} %get-tuple-element.39, bf16[256,2048]{1,0:T(8,128)(2,1)S(1)} %get-tuple-element.9, ...), kind=kOutput, calls=%fused_computation.34 | convolution fusion | flops 1618477056 | bytes 11544576 | tf_op jit(solution)/shard_map/project/dot_general | solution.py:114
  297.4 3.5 fusion.69
  305.2 6.2 %all-to-all-start.6 = ((f32[4,2,2048]{2,1,0:T(2,128)}), f32[4,2,2048]{2,1,0:T(2,128)S(1)}, u32[]{:S(2)}, u32[]{:S(2)}) async-start(f32[4,2,2048]{2,1,0:T(2,128)} %broadcast_in_dim.28), calls=%async_computation.6 | async-start | bytes 131072 | tf_op jit(solution)/shard_map/direction/all_to_all | solution.py:19
  312.4 7.1 %all-to-all-done.6 = f32[4,2,2048]{2,1,0:T(2,128)S(1)} async-done(((f32[4,2,2048]{2,1,0:T(2,128)}), f32[4,2,2048]{2,1,0:T(2,128)S(1)}, u32[]{:S(2)}, u32[]{:S(2)}) %all-to-all-start.6) | async-done | bytes 65568 | tf_op jit(solution)/shard_map/direction/all_to_all | solution.py:19
  320.4 15.3 %all-to-all-start.4 = ((f32[64,2,1024]{2,1,0:T(2,128)}), f32[64,2,1024]{2,1,0:T(2,128)S(1)}, u32[]{:S(2)}, u32[]{:S(2)}) async-start(f32[64,2,1024]{2,1,0:T(2,128)} %broadcast_in_dim.26), calls=%async_computation.4 | async-start | bytes 1048576 | tf_op jit(solution)/shard_map/tail/all_to_all | solution.py:19
  336.5 16.1 %all-to-all-done.4 = f32[64,2,1024]{2,1,0:T(2,128)S(1)} async-done(((f32[64,2,1024]{2,1,0:T(2,128)}), f32[64,2,1024]{2,1,0:T(2,128)S(1)}, u32[]{:S(2)}, u32[]{:S(2)}) %all-to-all-start.4) | async-done | bytes 524320 | tf_op jit(solution)/shard_map/tail/all_to_all | solution.py:19
  352.6 5.9 %all-to-all-start.7 = ((f32[64,2,128]{2,1,0:T(2,128)}), f32[64,2,128]{2,1,0:T(2,128)S(1)}, u32[]{:S(2)}, u32[]{:S(2)}) async-start(f32[64,2,128]{2,1,0:T(2,128)} %copy.57), calls=%async_computation.7 | async-start | bytes 131072 | tf_op jit(solution)/shard_map/direction/all_to_all | solution.py:102
  358.8 8.9 %all-to-all-done.7 = f32[64,2,128]{2,1,0:T(2,128)S(1)} async-done(((f32[64,2,128]{2,1,0:T(2,128)}), f32[64,2,128]{2,1,0:T(2,128)S(1)}, u32[]{:S(2)}, u32[]{:S(2)}) %all-to-all-start.7) | async-done | bytes 65568 | tf_op jit(solution)/shard_map/direction/all_to_all | solution.py:102
  368.4 3.3 all-to-all-start.9
  373.0 7.3 %all-to-all-done.9 = f32[4,64,128]{2,1,0:T(8,128)S(1)} async-done(((f32[4,64,128]{2,1,0:T(8,128)}), f32[4,64,128]{2,1,0:T(8,128)S(1)}, u32[]{:S(2)}, u32[]{:S(2)}) %all-to-all-start.9) | async-done | bytes 131104 | tf_op jit(solution)/shard_map/tail/all_to_all | solution.py:19
  380.3 6.4 %all-to-all-start.8 = ((f32[64,1,1024]{2,1,0:T(1,128)}), f32[64,1,1024]{2,1,0:T(1,128)S(1)}, u32[]{:S(2)}, u32[]{:S(2)}) async-start(f32[64,1,1024]{2,1,0:T(1,128)} %copy.59), calls=%async_computation.8 | async-start | bytes 524288 | tf_op jit(solution)/shard_map/direction/all_to_all | solution.py:107
  388.2 10.1 %all-to-all-done.8 = f32[64,1,1024]{2,1,0:T(1,128)S(1)} async-done(((f32[64,1,1024]{2,1,0:T(1,128)}), f32[64,1,1024]{2,1,0:T(1,128)S(1)}, u32[]{:S(2)}, u32[]{:S(2)}) %all-to-all-start.8) | async-done | bytes 262176 | tf_op jit(solution)/shard_map/direction/all_to_all | solution.py:107
  398.4 6.0 %all-to-all-start.10 = ((f32[64,1,1152]{2,1,0:T(1,128)}), f32[64,1,1152]{2,1,0:T(1,128)S(1)}, u32[]{:S(2)}, u32[]{:S(2)}) async-start(f32[64,1,1152]{2,1,0:T(1,128)} %copy.62), calls=%async_computation.10 | async-start | bytes 589824 | tf_op jit(solution)/shard_map/tail/all_to_all | solution.py:157
  404.9 11.3 %all-to-all-done.10 = f32[64,1,1152]{2,1,0:T(1,128)S(1)} async-done(((f32[64,1,1152]{2,1,0:T(1,128)}), f32[64,1,1152]{2,1,0:T(1,128)S(1)}, u32[]{:S(2)}, u32[]{:S(2)}) %all-to-all-start.10) | async-done | bytes 294944 | tf_op jit(solution)/shard_map/tail/all_to_all | solution.py:157
  (137 shorter events, 52.0 us)
Async XLA Ops:
  7.2 351.5 %copy-start = (bf16[1024,128]{1,0:T(8,128)(2,1)S(1)}, bf16[1024,128]{1,0:T(8,128)(2,1)}, u32[]{:S(2)}) copy-start(bf16[1024,128]{1,0:T(8,128)(2,1)} %param.15) | copy-start | bytes 786436
  7.2 10.8 %copy-start.20 = (s32[64]{0:T(128)S(1)}, s32[64]{0:T(128)}, u32[]{:S(2)}) copy-start(s32[64]{0:T(128)} %param.19) | copy-start | bytes 772
  7.2 10.8 %copy-start.21 = (s32[64]{0:T(128)S(1)}, s32[64]{0:T(128)}, u32[]{:S(2)}) copy-start(s32[64]{0:T(128)} %param.18) | copy-start | bytes 772
  7.2 65.5 %all-gather.3.cloned.1.call-start = ((), (), s32[]{:S(2)}) async-start(), calls=%async_computation.11 | async-start | bytes 1966080 | tf_op jit(solution)/shard_map/weights/all_gather | solution.py:70
  9.1 3.0 collective-permute-start.3
  9.8 7.3 %collective-permute-start.4 = (bf16[128,768]{1,0:T(8,128)(2,1)S(1)}, bf16[128,768]{1,0:T(8,128)(2,1)S(1)}, u32[]{:S(2)}, u32[]{:S(2)}) collective-permute-start(bf16[128,768]{1,0:T(8,128)(2,1)S(1)} %get-tuple-element.38), channel_id=1, source_target_pairs={{0,4},{1,12},{4,0},{5,8},{8,5},{9,13},{12,1},{13,9},{2,6},{3,14},{... | collective-permute-start | bytes 589832 | tf_op jit(solution)/shard_map/weights/ppermute | solution.py:31
  22.4 51.8 %all-to-all-start.5 = ((f32[64,1,2048]{2,1,0:T(1,128)}), f32[64,1,2048]{2,1,0:T(1,128)S(1)}, u32[]{:S(2)}, u32[]{:S(2)}) async-start(f32[64,1,2048]{2,1,0:T(1,128)} %copy.55), calls=%async_computation.5 | async-start | bytes 1048576 | tf_op jit(solution)/shard_map/direction/all_to_all | solution.py:98
  161.7 4.6 %copy-start.10 = (bf16[256,2048]{1,0:T(8,128)(2,1)S(1)}, bf16[256,2048]{1,0:T(8,128)(2,1)}, u32[]{:S(2)}) copy-start(bf16[256,2048]{1,0:T(8,128)(2,1)} %param.10) | copy-start | bytes 3145732
  161.7 16.6 %copy-start.13 = (bf16[8192]{0:T(1024)(128)(2,1)S(1)}, bf16[8192]{0:T(1024)(128)(2,1)}, u32[]{:S(2)}) copy-start(bf16[8192]{0:T(1024)(128)(2,1)} %param.11) | copy-start | bytes 49156
  161.7 66.7 %all-to-all-start = ((bf16[8,256,768]{2,1,0:T(8,128)(2,1)}), bf16[8,256,768]{2,1,0:T(8,128)(2,1)}, u32[]{:S(2)}, u32[]{:S(2)}) async-start(bf16[8,256,768]{2,1,0:T(8,128)(2,1)} %stack.16), calls=%async_computation | async-start | bytes 6291456 | tf_op jit(solution)/shard_map/weights/all_to_all | solution.py:74
  166.3 29.7 %collective-permute-start.6 = (bf16[256,2048]{1,0:T(8,128)(2,1)S(1)}, bf16[256,2048]{1,0:T(8,128)(2,1)}, u32[]{:S(2)}, u32[]{:S(2)}) collective-permute-start(bf16[256,2048]{1,0:T(8,128)(2,1)S(1)} %copy-done.10), channel_id=1, source_target_pairs={{0,2},{2,0},{1,3},{3,1},{4,6},{6,4},{5,7},{7,5},{8,10},{10,8},{9,1... | collective-permute-start | bytes 3145736 | tf_op jit(solution)/shard_map/tokens/ppermute | solution.py:88
  171.0 26.7 %collective-permute-start.5 = (bf16[256,2048]{1,0:T(8,128)(2,1)S(1)}, bf16[256,2048]{1,0:T(8,128)(2,1)}, u32[]{:S(2)}, u32[]{:S(2)}) collective-permute-start(bf16[256,2048]{1,0:T(8,128)(2,1)S(1)} %copy-done.10), channel_id=1, source_target_pairs={{1,9},{5,13},{9,1},{13,5},{3,11},{7,15},{11,3},{15,7},{17,25},{21,... | collective-permute-start | bytes 3145736 | tf_op jit(solution)/shard_map/tokens/ppermute | solution.py:31
  172.6 27.2 %collective-permute-start = (bf16[256,2048]{1,0:T(8,128)(2,1)S(1)}, bf16[256,2048]{1,0:T(8,128)(2,1)}, u32[]{:S(2)}, u32[]{:S(2)}) collective-permute-start(bf16[256,2048]{1,0:T(8,128)(2,1)S(1)} %copy-done.10), channel_id=1, source_target_pairs={{0,9},{1,0},{4,13},{5,4},{8,1},{9,8},{12,5},{13,12},{2,11},{3,2},{... | collective-permute-start | bytes 3145736 | tf_op jit(solution)/shard_map/tokens/ppermute | solution.py:31
  175.8 48.6 %collective-permute-start.2 = (bf16[256,2048]{1,0:T(8,128)(2,1)S(1)}, bf16[256,2048]{1,0:T(8,128)(2,1)}, u32[]{:S(2)}, u32[]{:S(2)}) collective-permute-start(bf16[256,2048]{1,0:T(8,128)(2,1)S(1)} %copy-done.10), channel_id=1, source_target_pairs={{0,5},{1,12},{4,9},{5,0},{8,13},{9,4},{12,1},{13,8},{2,7},{3,14},{... | collective-permute-start | bytes 3145736 | tf_op jit(solution)/shard_map/tokens/ppermute | solution.py:31
  175.8 49.3 %collective-permute-start.1 = (bf16[256,2048]{1,0:T(8,128)(2,1)S(1)}, bf16[256,2048]{1,0:T(8,128)(2,1)}, u32[]{:S(2)}, u32[]{:S(2)}) collective-permute-start(bf16[256,2048]{1,0:T(8,128)(2,1)S(1)} %copy-done.10), channel_id=1, source_target_pairs={{0,12},{1,5},{4,0},{5,9},{8,4},{9,13},{12,8},{13,1},{2,14},{3,7},{... | collective-permute-start | bytes 3145736 | tf_op jit(solution)/shard_map/tokens/ppermute | solution.py:31
  196.1 70.0 %collective-permute-start.10 = (bf16[256,2048]{1,0:T(8,128)(2,1)}, bf16[256,2048]{1,0:T(8,128)(2,1)}, u32[]{:S(2)}, u32[]{:S(2)}) collective-permute-start(bf16[256,2048]{1,0:T(8,128)(2,1)} %collective-permute-done.6), channel_id=1, source_target_pairs={{1,9},{5,13},{9,1},{13,5},{3,11},{7,15},{11,3},{15,7},{17,25},{21,... | collective-permute-start | bytes 3145736 | tf_op jit(solution)/shard_map/tokens/ppermute | solution.py:31
  197.7 66.5 %collective-permute-start.9 = (bf16[256,2048]{1,0:T(8,128)(2,1)}, bf16[256,2048]{1,0:T(8,128)(2,1)}, u32[]{:S(2)}, u32[]{:S(2)}) collective-permute-start(bf16[256,2048]{1,0:T(8,128)(2,1)} %collective-permute-done.6), channel_id=1, source_target_pairs={{0,5},{1,12},{4,9},{5,0},{8,13},{9,4},{12,1},{13,8},{2,7},{3,14},{... | collective-permute-start | bytes 3145736 | tf_op jit(solution)/shard_map/tokens/ppermute | solution.py:31
  199.8 64.5 %collective-permute-start.8 = (bf16[256,2048]{1,0:T(8,128)(2,1)}, bf16[256,2048]{1,0:T(8,128)(2,1)}, u32[]{:S(2)}, u32[]{:S(2)}) collective-permute-start(bf16[256,2048]{1,0:T(8,128)(2,1)} %collective-permute-done.6), channel_id=1, source_target_pairs={{0,12},{1,5},{4,0},{5,9},{8,4},{9,13},{12,8},{13,1},{2,14},{3,7},{... | collective-permute-start | bytes 3145736 | tf_op jit(solution)/shard_map/tokens/ppermute | solution.py:31
  202.3 24.5 %copy-start.1 = (bf16[256,2048]{1,0:T(8,128)(2,1)}, bf16[256,2048]{1,0:T(8,128)(2,1)S(1)}, u32[]{:S(2)}) copy-start(bf16[256,2048]{1,0:T(8,128)(2,1)S(1)} %get-tuple-element.24) | copy-start | bytes 3145732
  202.3 24.5 %copy-start.3 = (bf16[256,2048]{1,0:T(8,128)(2,1)}, bf16[256,2048]{1,0:T(8,128)(2,1)S(1)}, u32[]{:S(2)}) copy-start(bf16[256,2048]{1,0:T(8,128)(2,1)S(1)} %get-tuple-element.23) | copy-start | bytes 3145732
  224.4 41.7 %collective-permute-start.7 = (bf16[256,2048]{1,0:T(8,128)(2,1)}, bf16[256,2048]{1,0:T(8,128)(2,1)}, u32[]{:S(2)}, u32[]{:S(2)}) collective-permute-start(bf16[256,2048]{1,0:T(8,128)(2,1)} %collective-permute-done.6), channel_id=1, source_target_pairs={{0,9},{1,0},{4,13},{5,4},{8,1},{9,8},{12,5},{13,12},{2,11},{3,2},{... | collective-permute-start | bytes 3145736 | tf_op jit(solution)/shard_map/tokens/ppermute | solution.py:31
  230.3 50.8 %all-to-all-start.3 = ((bf16[8,256,768]{2,1,0:T(8,128)(2,1)}), bf16[8,256,768]{2,1,0:T(8,128)(2,1)}, u32[]{:S(2)}, u32[]{:S(2)}) async-start(bf16[8,256,768]{2,1,0:T(8,128)(2,1)} %stack.19), calls=%async_computation.3 | async-start | bytes 6291456 | tf_op jit(solution)/shard_map/weights/all_to_all | solution.py:74
  276.1 5.0 %copy-start.6 = (bf16[256,2048]{1,0:T(8,128)(2,1)S(1)}, bf16[256,2048]{1,0:T(8,128)(2,1)}, u32[]{:S(2)}) copy-start(bf16[256,2048]{1,0:T(8,128)(2,1)} %copy-done.5) | copy-start | bytes 3145732
  300.9 3.7 copy-start.19
  303.1 8.3 %collective-permute-start.12 = (bf16[256,512]{1,0:T(8,128)(2,1)S(1)}, bf16[256,512]{1,0:T(8,128)(2,1)S(1)}, u32[]{:S(2)}, u32[]{:S(2)}) collective-permute-start(bf16[256,512]{1,0:T(8,128)(2,1)S(1)} %copy.54), channel_id=1, source_target_pairs={{0,4},{1,12},{4,8},{5,0},{8,13},{9,5},{12,1},{13,9},{2,6},{3,14},{... | collective-permute-start | bytes 786440 | tf_op jit(solution)/shard_map/return_heads/ppermute | solution.py:31
  303.9 7.6 %collective-permute-start.11 = (bf16[256,512]{1,0:T(8,128)(2,1)S(1)}, bf16[256,512]{1,0:T(8,128)(2,1)S(1)}, u32[]{:S(2)}, u32[]{:S(2)}) collective-permute-start(bf16[256,512]{1,0:T(8,128)(2,1)S(1)} %copy.53), channel_id=1, source_target_pairs={{0,0},{1,8},{4,4},{5,12},{8,9},{9,1},{12,13},{13,5},{2,2},{3,10},{... | collective-permute-start | bytes 786440 | tf_op jit(solution)/shard_map/return_heads/ppermute | solution.py:31
  305.2 14.2 %all-to-all-start.6 = ((f32[4,2,2048]{2,1,0:T(2,128)}), f32[4,2,2048]{2,1,0:T(2,128)S(1)}, u32[]{:S(2)}, u32[]{:S(2)}) async-start(f32[4,2,2048]{2,1,0:T(2,128)} %broadcast_in_dim.28), calls=%async_computation.6 | async-start | bytes 131072 | tf_op jit(solution)/shard_map/direction/all_to_all | solution.py:19
  320.4 32.2 %all-to-all-start.4 = ((f32[64,2,1024]{2,1,0:T(2,128)}), f32[64,2,1024]{2,1,0:T(2,128)S(1)}, u32[]{:S(2)}, u32[]{:S(2)}) async-start(f32[64,2,1024]{2,1,0:T(2,128)} %broadcast_in_dim.26), calls=%async_computation.4 | async-start | bytes 1048576 | tf_op jit(solution)/shard_map/tail/all_to_all | solution.py:19
  352.6 15.2 %all-to-all-start.7 = ((f32[64,2,128]{2,1,0:T(2,128)}), f32[64,2,128]{2,1,0:T(2,128)S(1)}, u32[]{:S(2)}, u32[]{:S(2)}) async-start(f32[64,2,128]{2,1,0:T(2,128)} %copy.57), calls=%async_computation.7 | async-start | bytes 131072 | tf_op jit(solution)/shard_map/direction/all_to_all | solution.py:102
  368.4 11.8 %all-to-all-start.9 = ((f32[4,64,128]{2,1,0:T(8,128)}), f32[4,64,128]{2,1,0:T(8,128)S(1)}, u32[]{:S(2)}, u32[]{:S(2)}) async-start(f32[4,64,128]{2,1,0:T(8,128)} %broadcast_in_dim.30), calls=%async_computation.9 | async-start | bytes 262144 | tf_op jit(solution)/shard_map/tail/all_to_all | solution.py:19
  380.3 18.1 %all-to-all-start.8 = ((f32[64,1,1024]{2,1,0:T(1,128)}), f32[64,1,1024]{2,1,0:T(1,128)S(1)}, u32[]{:S(2)}, u32[]{:S(2)}) async-start(f32[64,1,1024]{2,1,0:T(1,128)} %copy.59), calls=%async_computation.8 | async-start | bytes 524288 | tf_op jit(solution)/shard_map/direction/all_to_all | solution.py:107
  398.4 17.8 %all-to-all-start.10 = ((f32[64,1,1152]{2,1,0:T(1,128)}), f32[64,1,1152]{2,1,0:T(1,128)S(1)}, u32[]{:S(2)}, u32[]{:S(2)}) async-start(f32[64,1,1152]{2,1,0:T(1,128)} %copy.62), calls=%async_computation.10 | async-start | bytes 589824 | tf_op jit(solution)/shard_map/tail/all_to_all | solution.py:157
  (13 other events, 30.8 us)
Sparse Core Ops, SparseCore 0:
  18.0 54.5 all-gather.2
